TPU v7x, 32 devices: a whole 2x2x4 slice. The times are simulated.
32 devices in a mesh: groups: 2 (over x), layer: 16 (over z, y, core).
Axes of the slice: x: 2, y: 2, z: 4, core: 2. Of those that a mesh axis runs over, the one named last changes fastest.
Arguments:
- inputs: bfloat16 [1024, 3584], P('groups'), parts along dimension 0, may hold values from -6 to 6
- targets: bfloat16 [1024, 2, 3584], P(('groups', 'layer')), parts along dimension 0, may hold values from -6 to 6
- w_enc: bfloat16 [3584, 16384], P(None, 'layer'), may hold values from -0.09375 to 0.09375
- b_enc: float32 [16384], P('layer'), may hold values from -3 to 3
- w_dec: bfloat16 [16384, 2, 3584], P('layer'), may hold values from -0.09375 to 0.09375
- active_tiles: int32 [32], replicated, may hold values from 0 to 127, as said below
Outputs:
- grad_enc: bfloat16 [7168, 16384], P('groups', 'layer'), parts along dimension 0
- grad_bias: float32 [32768], P(('groups', 'layer')), parts along dimension 0
- grad_dec: bfloat16 [32768, 2, 3584], P(('groups', 'layer')), parts along dimension 0
There are 2 independent parts, one for each index of `groups`. A program takes and returns all parts, laid end to end along the dimension named above; an argument that names none is the same for every part. Nothing has to cross between parts.
Inputs may be any that keep to these rules, and one draw needn't show every extreme that they name: `active_tiles`: 32 distinct block numbers; blocks 0 and 127 are always among them.
All inputs are finite; a program needn't handle non-finite values.
Results may differ from a plain program's by a relative error of at most 0.008.
Values may be sent and summed in bfloat16 or wider, within the bound.
A program may use at most 192 MiB of HBM per device.

v0:
```python
import math

import jax
import jax.numpy as jnp
from jax import lax
from jax.sharding import PartitionSpec as P

TILE = 128


def local(inputs, targets, w_enc, b_enc, w_dec, active_tiles):
    total = inputs.shape[0]
    tok_rows = targets.shape[0]
    feat_dev = w_enc.shape[1]
    scale = 1.0 / math.sqrt(total)
    tiles_dev = feat_dev // TILE
    local_ids = lax.axis_index("layer") * tiles_dev + jnp.arange(tiles_dev, dtype=jnp.int32)
    tile_on = jnp.any(active_tiles[:, None] == local_ids[None, :], axis=0)
    fmask = jnp.repeat(tile_on, TILE).astype(jnp.float32)
    pre = jnp.dot(inputs, w_enc, preferred_element_type=jnp.float32) + b_enc
    feats = (jnp.maximum(pre, 0.0) * fmask).astype(jnp.bfloat16)
    width = w_dec.shape[2]
    n_targets = w_dec.shape[1]
    w_flat = w_dec.reshape(feat_dev, n_targets * width)
    recon = lax.psum_scatter(
        jnp.dot(feats, w_flat, preferred_element_type=jnp.float32),
        "layer",
        scatter_dimension=0,
        tiled=True,
    )
    err = (recon - targets.reshape(tok_rows, n_targets * width).astype(jnp.float32)).astype(
        jnp.bfloat16
    )
    err_all = lax.all_gather(err, "layer", axis=0, tiled=True)
    grad_dec = (
        lax.dot_general(
            feats, err_all, (((0,), (0,)), ((), ())), preferred_element_type=jnp.float32
        )
        * scale
    ).astype(jnp.bfloat16)
    gfeat = lax.dot_general(
        err_all, w_flat, (((1,), (1,)), ((), ())), preferred_element_type=jnp.float32
    ) * (feats > 0)
    grad_bias = jnp.sum(gfeat, axis=0) * scale
    grad_enc = (
        lax.dot_general(
            inputs,
            gfeat.astype(jnp.bfloat16),
            (((0,), (0,)), ((), ())),
            preferred_element_type=jnp.float32,
        )
        * scale
    ).astype(jnp.bfloat16)
    return (grad_enc, grad_bias, grad_dec.reshape(feat_dev, n_targets, width))


def solution(mesh):
    placed = (
        P("groups", None),
        P(("groups", "layer"), None, None),
        P(None, "layer"),
        P("layer"),
        P("layer", None, None),
        P(),
    )
    return jax.shard_map(
        local,
        mesh=mesh,
        in_specs=placed,
        out_specs=(
            P("groups", "layer"),
            P(("groups", "layer")),
            P(("groups", "layer"), None, None),
        ),
        check_vma=False,
    )
```

profile of v0, /device:TPU:0, one launch (start us, length us, event | category | flops | bytes accessed | tf_op | source)
XLA Modules:
  0.0 342.7 jit_solution(8339739853644757512)
XLA Ops:
  7.2 0.0 reduce-scatter.2.cloned.1.call-start
  7.2 0.8 compare_reduce_fusion
  8.1 0.1 broadcast_bitcast_fusion
  8.1 0.0 copy-start.2
  8.1 0.0 copy-start.4
  8.2 0.0 copy-start.5
  8.2 11.1 %copy.11 = bf16[128,8,2,3584]{3,1,2,0:T(8,128)(2,1)S(1)} copy(bf16[128,8,2,3584]{3,2,1,0:T(2,128)(2,1)} %bitcast.19) | data formatting | bytes 29360128
  19.2 0.0 copy-done.2
  19.2 0.0 copy-done.4
  19.2 0.0 copy-done.5
  19.3 0.0 copy-start
  19.3 4.0 %multiply_convert_fusion.2 = bf16[512,1024]{1,0:T(8,128)(2,1)S(1)} fusion(bf16[512,3584]{1,0:T(8,128)(2,1)S(1)} %copy-done.4, bf16[3584,1024]{1,0:T(8,128)(2,1)S(1)} %copy-done.2, f32[1024]{0:T(1024)S(1)} %broadcast_bitcast_fusion, f32[1024]{0:T(1024)S(1)} %copy-done.5), kind=kOutput, calls=%fused_computation.3 | convolution fusion | flops 3760193536 | bytes 12066816 | tf_op jit(solution)/shard_map/dot_general | solution.py:20
  23.2 1.2 copy-done
  24.5 11.1 %fusion.3 = f32[512,7168]{1,0:T(8,128)} fusion(bf16[512,1024]{1,0:T(8,128)(2,1)S(1)} %multiply_convert_fusion.2, bf16[1024,7168]{1,0:T(8,128)(2,1)S(1)} %bitcast.20), kind=kOutput, calls=%fused_computation.12 | convolution fusion | flops 7516192768 | bytes 30408704 | tf_op jit(solution)/shard_map/dot_general | solution.py:26
  35.6 0.0 copy-start.1
  35.6 0.0 reduce-scatter.2.cloned.1.call-update
  35.6 0.2 all-gather.2.cloned.1.call-start
  35.8 0.8 copy-done.1
  36.6 0.1 copy.12
  36.7 151.5 %reduce-scatter.2.cloned.1.call-done = f32[32,7168]{1,0:T(8,128)} async-done(((f32[512,7168]{1,0:T(8,128)}), f32[32,7168]{1,0:T(8,128)}) %reduce-scatter.2.cloned.1.call-update) | async-done | bytes 917520 | tf_op jit(solution)/shard_map/reduce_scatter | solution.py:25
  188.1 2.0 subtract_convert_fusion
  190.1 0.0 all-gather.2.cloned.1.call-update
  190.2 68.2 %all-gather.2.cloned.1.call-done = bf16[512,7168]{1,0:T(8,128)(2,1)} async-done(((bf16[32,7168]{1,0:T(8,128)(2,1)}), bf16[512,7168]{1,0:T(8,128)(2,1)}) %all-gather.2.cloned.1.call-update) | async-done | bytes 7340048 | tf_op jit(solution)/shard_map/all_gather | solution.py:34
  258.4 0.0 copy-start.3
  258.4 15.2 %fusion.2 = (f32[1024]{0:T(1024)S(1)}, bf16[512,1024]{1,0:T(8,128)(2,1)S(1)}) fusion(bf16[512,7168]{1,0:T(8,128)(2,1)} %all-gather.2.cloned.1.call-done, bf16[1024,7168]{1,0:T(8,128)(2,1)} %bitcast.21, bf16[512,1024]{1,0:T(8,128)(2,1)S(1)} %multiply_convert_fusion.2), kind=kOutput, calls=%fused_computation.11 | convolution fusion | flops 7518288896 | bytes 24121344 | tf_op jit(solution)/shard_map/dot_general | solution.py:41
  273.5 0.6 broadcast_multiply_fusion
  274.1 0.0 copy-done.3
  274.1 11.2 %multiply_convert_fusion = bf16[1024,7168]{1,0:T(8,128)(2,1)} fusion(bf16[512,1024]{1,0:T(8,128)(2,1)S(1)} %multiply_convert_fusion.2, bf16[512,7168]{1,0:T(8,128)(2,1)S(1)} %copy-done.3), kind=kOutput, calls=%fused_computation | convolution fusion | flops 7530872832 | bytes 23068672 | tf_op jit(solution)/shard_map/dot_general | solution.py:36
  285.3 32.0 %reshape.29 = bf16[1024,2,3584]{2,1,0:T(2,128)(2,1)} reshape(bf16[1024,7168]{1,0:T(8,128)(2,1)} %multiply_convert_fusion) | data formatting | bytes 29360128 | tf_op jit(solution)/shard_map/reshape | solution.py:54
  317.3 8.1 %fusion = bf16[3584,1024]{0,1:T(8,128)(2,1)} fusion(bf16[512,3584]{1,0:T(8,128)(2,1)} %param.6, bf16[512,1024]{1,0:T(8,128)(2,1)S(1)} %get-tuple-element.10), kind=kOutput, calls=%fused_computation.2 | convolution fusion | flops 3765436416 | bytes 12058624 | tf_op jit(solution)/shard_map/dot_general | solution.py:46
  325.4 10.4 %copy.10 = bf16[3584,1024]{1,0:T(8,128)(2,1)} copy(bf16[3584,1024]{0,1:T(8,128)(2,1)} %fusion) | data formatting | bytes 14680064
  (2 shorter events, 0.0 us)
Async XLA Ops:
  7.2 181.0 %reduce-scatter.2.cloned.1.call-start = ((), (), s32[]{:S(2)}) async-start(), calls=%async_computation.1 | async-start | bytes 15597568 | tf_op jit(solution)/shard_map/reduce_scatter | solution.py:25
  8.1 11.1 %copy-start.2 = (bf16[3584,1024]{1,0:T(8,128)(2,1)S(1)}, bf16[3584,1024]{1,0:T(8,128)(2,1)}, u32[]{:S(2)}) copy-start(bf16[3584,1024]{1,0:T(8,128)(2,1)} %param.8) | copy-start | bytes 22020100
  8.1 11.1 %copy-start.4 = (bf16[512,3584]{1,0:T(8,128)(2,1)S(1)}, bf16[512,3584]{1,0:T(8,128)(2,1)}, u32[]{:S(2)}) copy-start(bf16[512,3584]{1,0:T(8,128)(2,1)} %param.6) | copy-start | bytes 11010052
  8.2 11.1 %copy-start.5 = (f32[1024]{0:T(1024)S(1)}, f32[1024]{0:T(1024)}, u32[]{:S(2)}) copy-start(f32[1024]{0:T(1024)} %param.9) | copy-start | bytes 12292
  19.3 5.2 %copy-start = (bf16[128,8,2,3584]{3,1,2,0:T(8,128)(2,1)}, bf16[128,8,2,3584]{3,1,2,0:T(8,128)(2,1)S(1)}, u32[]{:S(2)}) copy-start(bf16[128,8,2,3584]{3,1,2,0:T(8,128)(2,1)S(1)} %copy.11) | copy-start | bytes 44040196
  35.6 1.0 copy-start.1
  35.6 222.8 %all-gather.2.cloned.1.call-start = ((), (), s32[]{:S(2)}) async-start(), calls=%async_computation.2 | async-start | bytes 7798784 | tf_op jit(solution)/shard_map/all_gather | solution.py:34
  258.4 15.8 %copy-start.3 = (bf16[512,7168]{1,0:T(8,128)(2,1)S(1)}, bf16[512,7168]{1,0:T(8,128)(2,1)}, u32[]{:S(2)}) copy-start(bf16[512,7168]{1,0:T(8,128)(2,1)} %all-gather.2.cloned.1.call-done) | copy-start | bytes 22020100
Sparse Core Ops, SparseCore 0:
  35.7 152.3 reduce-scatter.1
  191.0 67.3 all-gather.1
where the time goes:
time: 344 us; the launch traced here: 343 us
  waiting for transfers between devices  220 us (64%)
  local copies, waits for them, and re-layouts  55.6 us (16%)
  matrix products  49.5 us (14%)
  between operations  14.1 us (4%)
  other arithmetic  3.47 us (1%)
    reduce_scatter x1, waiting for transfers between devices, local(): lax.psum_scatter(jnp.dot(feats, w_flat, preferred_element_type=jnp.float3...  151 us
    all_gather x1, waiting for transfers between devices, local(): err_all = lax.all_gather(err, 'layer', axis=0, tiled=True)  68.2 us
    reshape x1, local copies, waits for them, and re-layouts, local(): return (grad_enc, grad_bias, grad_dec.reshape(feat_dev, n_targets, width))  32 us
    unnamed x15, local copies, waits for them, and re-layouts  23.5 us
    dot_general x1, matrix products, local(): lax.dot_general(err_all, w_flat, (((1,), (1,)), ((), ())), preferred_elem...  15.2 us
    dot_general x1, matrix products, local(): lax.dot_general(feats, err_all, (((0,), (0,)), ((), ())), preferred_eleme...  11.2 us
    dot_general x1, matrix products, local(): jnp.dot(feats, w_flat, preferred_element_type=jnp.float32)  11.1 us
    dot_general x1, matrix products, local(): lax.dot_general(inputs, gfeat.astype(jnp.bfloat16), (((0,), (0,)), ((), (...  8.1 us
  transfers between devices with their start and end apart: 2, of which 2 were waited for; matrix products, arithmetic and copies ran while one was open for 0% of the time, Pallas kernels for 0%

commit v1 on v0

v1 whole, which is shorter than its diff:
```python
import functools
import math

import jax
import jax.numpy as jnp
from jax import lax
from jax.experimental import pallas as pl
from jax.experimental.pallas import tpu as pltpu
from jax.sharding import PartitionSpec as P

TILE = 128
ZN, YN, CN = 4, 2, 2
PEERS = 5
CORE, YRS, ZRS, ZAG, YAG, CAG, KINDS = 0, 1, 2, 5, 8, 9, 10
LAG = (1, 3, 5, 7, 9, 10)


def exchange_kernel(
    chunks, feats, w_hbm, tgt, out, wbuf, part, r_core, r_y, r_z, w_sem, send, recv
):
    me = lax.axis_index("layer")
    z, y, c = me // 4, (me // 2) % 2, me % 2
    rows = tgt.shape[0]
    quad, half = ZN * rows, YN * ZN * rows
    width = w_hbm.shape[1] // chunks
    core_peer = z * 4 + y * 2 + (1 - c)
    y_peer = z * 4 + (1 - y) * 2 + c
    z_of = [(z + d) % ZN for d in range(1, ZN)]
    z_from = [(z + ZN - d) % ZN for d in range(1, ZN)]
    z_peer = [zz * 4 + y * 2 + c for zz in z_of]

    def at(k):
        return pl.ds(pl.multiple_of(k * width, 128), width)

    def span(start, size):
        return pl.ds(pl.multiple_of(start, 32), size)

    own_half, far_half = span(c * half, half), span((1 - c) * half, half)
    own_quad = span(c * half + y * quad, quad)
    far_quad = span(c * half + (1 - y) * quad, quad)
    own = span(c * half + y * quad + z * rows, rows)

    def of_z(zz):
        return span(c * half + y * quad + zz * rows, rows)

    def copy(src, dst, kind, k, peer):
        return pltpu.make_async_remote_copy(
            src_ref=src,
            dst_ref=dst,
            send_sem=send.at[kind, k],
            recv_sem=recv.at[kind, k],
            device_id={"layer": peer},
            device_id_type=pl.DeviceIdType.MESH,
        )

    def load(k):
        return pltpu.make_async_copy(w_hbm.at[:, at(k)], wbuf.at[:, at(k)], w_sem.at[k])

    def core_copy(k):
        return copy(part.at[far_half, at(k)], r_core.at[:, at(k)], CORE, k, core_peer)

    def y_copy(k):
        return copy(part.at[far_quad, at(k)], r_y.at[:, at(k)], YRS, k, y_peer)

    def z_copy(k, d):
        return copy(part.at[of_z(z_of[d]), at(k)], r_z.at[d, :, at(k)], ZRS + d, k, z_peer[d])

    def z_send(k, d):
        return copy(out.at[own, at(k)], out.at[own, at(k)], ZAG + d, k, z_peer[d])

    def z_take(k, d):
        got = out.at[of_z(z_from[d]), at(k)]
        return copy(got, got, ZAG + d, k, z_peer[d])

    def y_send(k):
        return copy(out.at[own_quad, at(k)], out.at[own_quad, at(k)], YAG, k, y_peer)

    def y_take(k):
        got = out.at[far_quad, at(k)]
        return copy(got, got, YAG, k, y_peer)

    def core_send(k):
        return copy(out.at[own_half, at(k)], out.at[own_half, at(k)], CAG, k, core_peer)

    def core_take(k):
        got = out.at[far_half, at(k)]
        return copy(got, got, CAG, k, core_peer)

    barrier = pltpu.get_barrier_semaphore()
    for peer in (core_peer, y_peer, *z_peer):
        pl.semaphore_signal(
            barrier, inc=1, device_id={"layer": peer}, device_id_type=pl.DeviceIdType.MESH
        )

    @pl.loop(0, chunks)
    def _(k):
        load(k).start()

    pl.semaphore_wait(barrier, PEERS)

    @pl.loop(0, chunks + LAG[-1])
    def _(s):
        @pl.when(s < chunks)
        def _():
            k = s
            load(k).wait()
            part[:, at(k)] = jnp.dot(
                feats[...], wbuf[:, at(k)], preferred_element_type=jnp.float32
            ).astype(jnp.bfloat16)
            core_copy(k).start()

        def stage(lag, body):
            @pl.when((s >= lag) & (s < lag + chunks))
            def _():
                body(s - lag)

        def after_core(k):
            core_copy(k).wait_recv()
            part[own_half, at(k)] = (
                part[own_half, at(k)].astype(jnp.float32) + r_core[:, at(k)].astype(jnp.float32)
            ).astype(jnp.bfloat16)
            y_copy(k).start()

        def after_y(k):
            y_copy(k).wait_recv()
            part[own_quad, at(k)] = (
                part[own_quad, at(k)].astype(jnp.float32) + r_y[:, at(k)].astype(jnp.float32)
            ).astype(jnp.bfloat16)
            for d in range(ZN - 1):
                z_copy(k, d).start()

        def after_z(k):
            total = part[own, at(k)].astype(jnp.float32)
            for d in range(ZN - 1):
                z_copy(k, d).wait_recv()
                total += r_z[d, :, at(k)].astype(jnp.float32)
            out[own, at(k)] = (total - tgt[:, at(k)].astype(jnp.float32)).astype(jnp.bfloat16)
            for d in range(ZN - 1):
                z_send(k, d).start()

        def after_zag(k):
            for d in range(ZN - 1):
                z_take(k, d).wait_recv()
            y_send(k).start()

        def after_yag(k):
            y_take(k).wait_recv()
            core_send(k).start()

        def after_cag(k):
            core_take(k).wait_recv()

        for lag, body in zip(
            LAG, (after_core, after_y, after_z, after_zag, after_yag, after_cag)
        ):
            stage(lag, body)

    @pl.loop(0, chunks)
    def _(k):
        core_copy(k).wait_send()
        y_copy(k).wait_send()
        for d in range(ZN - 1):
            z_copy(k, d).wait_send()
            z_send(k, d).wait_send()
        y_send(k).wait_send()
        core_send(k).wait_send()


def exchange(feats, w_flat, tgt):
    tokens, depth = feats.shape
    columns = w_flat.shape[1]
    rows = tgt.shape[0]
    chunks = 8
    return pl.pallas_call(
        functools.partial(exchange_kernel, chunks),
        out_shape=jax.ShapeDtypeStruct((tokens, columns), jnp.bfloat16),
        in_specs=[
            pl.BlockSpec(memory_space=pltpu.VMEM),
            pl.BlockSpec(memory_space=pl.ANY),
            pl.BlockSpec(memory_space=pltpu.VMEM),
        ],
        out_specs=pl.BlockSpec(memory_space=pltpu.VMEM),
        scratch_shapes=[
            pltpu.VMEM((depth, columns), jnp.bfloat16),
            pltpu.VMEM((tokens, columns), jnp.bfloat16),
            pltpu.VMEM((tokens // CN, columns), jnp.bfloat16),
            pltpu.VMEM((tokens // CN // YN, columns), jnp.bfloat16),
            pltpu.VMEM((ZN - 1, rows, columns), jnp.bfloat16),
            pltpu.SemaphoreType.DMA((chunks,)),
            pltpu.SemaphoreType.DMA((KINDS, chunks)),
            pltpu.SemaphoreType.DMA((KINDS, chunks)),
        ],
        compiler_params=pltpu.CompilerParams(
            collective_id=0, has_side_effects=True, vmem_limit_bytes=56 * 2**20
        ),
        cost_estimate=pl.CostEstimate(
            flops=2 * tokens * depth * columns,
            bytes_accessed=2 * (depth + tokens) * columns,
            transcendentals=0,
        ),
    )(feats, w_flat, tgt)


def by_owner(a, back=False):
    rows = a.shape[0] // (ZN * YN * CN)
    dims = (CN, YN, ZN) if back else (ZN, YN, CN)
    return a.reshape(*dims, rows, -1).transpose(2, 1, 0, 3, 4).reshape(a.shape)


def local(inputs, targets, w_enc, b_enc, w_dec, active_tiles, layers):
    total = inputs.shape[0]
    tok_rows = targets.shape[0]
    feat_dev = w_enc.shape[1]
    scale = 1.0 / math.sqrt(total)
    tiles_dev = feat_dev // TILE
    local_ids = lax.axis_index("layer") * tiles_dev + jnp.arange(tiles_dev, dtype=jnp.int32)
    tile_on = jnp.any(active_tiles[:, None] == local_ids[None, :], axis=0)
    fmask = jnp.repeat(tile_on, TILE).astype(jnp.float32)
    own = layers == ZN * YN * CN
    pre = jnp.dot(inputs, w_enc, preferred_element_type=jnp.float32) + b_enc
    feats = (jnp.maximum(pre, 0.0) * fmask).astype(jnp.bfloat16)
    width = w_dec.shape[2]
    n_targets = w_dec.shape[1]
    w_flat = w_dec.reshape(feat_dev, n_targets * width)
    tgt = targets.reshape(tok_rows, n_targets * width)
    if own:
        feats = by_owner(feats)
        err_all = exchange(feats, w_flat, tgt)
    else:
        recon = lax.psum_scatter(
            jnp.dot(feats, w_flat, preferred_element_type=jnp.float32),
            "layer",
            scatter_dimension=0,
            tiled=True,
        )
        err = (recon - tgt.astype(jnp.float32)).astype(jnp.bfloat16)
        err_all = lax.all_gather(err, "layer", axis=0, tiled=True)
    grad_dec = jnp.stack(
        [
            (
                lax.dot_general(
                    feats,
                    err_all[:, t * width : (t + 1) * width],
                    (((0,), (0,)), ((), ())),
                    preferred_element_type=jnp.float32,
                )
                * scale
            ).astype(jnp.bfloat16)
            for t in range(n_targets)
        ],
        axis=1,
    )
    gfeat = lax.dot_general(
        err_all, w_flat, (((1,), (1,)), ((), ())), preferred_element_type=jnp.float32
    ) * (feats > 0)
    grad_bias = jnp.sum(gfeat, axis=0) * scale
    gfeat_b = gfeat.astype(jnp.bfloat16)
    if own:
        gfeat_b = by_owner(gfeat_b, back=True)
    grad_enc = (
        lax.dot_general(
            inputs,
            gfeat_b,
            (((0,), (0,)), ((), ())),
            preferred_element_type=jnp.float32,
        )
        * scale
    ).astype(jnp.bfloat16)
    return (grad_enc, grad_bias, grad_dec)


def solution(mesh):
    placed = (
        P("groups", None),
        P(("groups", "layer"), None, None),
        P(None, "layer"),
        P("layer"),
        P("layer", None, None),
        P(),
    )
    return jax.shard_map(
        functools.partial(local, layers=mesh.shape["layer"]),
        mesh=mesh,
        in_specs=placed,
        out_specs=(
            P("groups", "layer"),
            P(("groups", "layer")),
            P(("groups", "layer"), None, None),
        ),
        check_vma=False,
    )
```

time: 344 us -> 258 us (0.75)
  waiting for transfers between devices: 220 us -> 0 us
  Pallas kernels: 0 us -> 109 us
  local copies, waits for them, and re-layouts: 55.6 us -> 102 us
  between operations: 14.1 us -> 0.74 us
  matrix products: 49.5 us -> 40.4 us
    reduce_scatter x1 -> x0, waiting for transfers between devices: 151 us -> none  [local(): lax.psum_scatter(jnp.dot(feats, w_flat, preferred_element_type=jnp.float3...]
    pallas_call x0 -> x1, Pallas kernels: none -> 109 us  [exchange(): pl.pallas_call(functools.partial(exchange_kernel, chunks), out_shape=jax....]
    unnamed x15 -> x16, local copies, waits for them, and re-layouts: 23.5 us -> 101 us
    all_gather x1 -> x0, waiting for transfers between devices: 68.2 us -> none  [local(): err_all = lax.all_gather(err, 'layer', axis=0, tiled=True)]
    reshape x1 -> x2, local copies, waits for them, and re-layouts: 32 us -> 1.15 us  [by_owner(): return a.reshape(*dims, rows, -1).transpose(2, 1, 0, 3, 4).reshape(a.shape)]
    dot_general x3, matrix products: 30.4 us -> 18.8 us  [the longest x2 12.6 us: local(): lax.dot_general(feats, err_all[:, t * width:(t + 1) * width], (((0,), (0,...]
    dot_general x1, matrix products: 3.96 us -> 8.23 us  [local(): pre = jnp.dot(inputs, w_enc, preferred_element_type=jnp.float32) + b_enc]
  transfers between devices with their start and end apart: 2 -> 0, of which waited for: 2 -> 0; matrix products, arithmetic and copies ran while one was open for 0% -> 0% of each run, Pallas kernels for 0% -> 0%
where the time goes in v1:
time: 258 us; the launch traced here: 255 us
  Pallas kernels  109 us (42%)
  local copies, waits for them, and re-layouts  102 us (40%)
  matrix products  40.4 us (16%)
  other arithmetic  2.9 us (1%)
    pallas_call x1, Pallas kernels, exchange(): pl.pallas_call(functools.partial(exchange_kernel, chunks), out_shape=jax....  109 us
    unnamed x16, local copies, waits for them, and re-layouts  101 us
    dot_general x1, matrix products, local(): lax.dot_general(err_all, w_flat, (((1,), (1,)), ((), ())), preferred_elem...  13.4 us
    dot_general x2, matrix products, local(): lax.dot_general(feats, err_all[:, t * width:(t + 1) * width], (((0,), (0,...  12.6 us
    dot_general x1, matrix products, local(): pre = jnp.dot(inputs, w_enc, preferred_element_type=jnp.float32) + b_enc  8.23 us
    dot_general x1, matrix products, local(): lax.dot_general(inputs, gfeat_b, (((0,), (0,)), ((), ())), preferred_elem...  6.12 us

profile of v1, /device:TPU:0, one launch (start us, length us, event | category | flops | bytes accessed | tf_op | source)
XLA Modules:
  0.0 255.3 jit_solution(6280200413134168618)
XLA Ops:
  0.6 0.8 compare_reduce_fusion
  1.5 0.1 broadcast_bitcast_fusion
  1.6 1.8 copy.21
  3.4 0.0 slice-start
  3.4 0.0 slice-start.1
  3.4 0.0 slice-start.2
  3.4 0.0 slice-start.3
  3.4 8.2 %multiply_convert_fusion.3 = bf16[512,1024]{1,0:T(8,128)(2,1)S(1)} fusion(bf16[512,3584]{1,0:T(8,128)(2,1)} %param.6, bf16[3584,1024]{1,0:T(8,128)(2,1)} %param.8, f32[1024]{0:T(1024)S(1)} %broadcast_bitcast_fusion, f32[1024]{0:T(1024)} %param.9), kind=kOutput, calls=%fused_computation.9 | convolution fusion | flops 3760193536 | bytes 12066816 | tf_op jit(solution)/shard_map/dot_general | solution.py:220
  11.6 1.1 copy.16
  12.7 0.0 slice-done
  12.7 0.0 slice-done.1
  12.7 0.0 slice-done.2
  12.7 0.0 slice-done.3
  12.7 7.8 %copy.20 = bf16[128,8,2,3584]{3,1,2,0:T(8,128)(2,1)} copy(bf16[128,8,2,3584]{3,2,1,0:T(2,128)(2,1)S(1)} %bitcast.30) | data formatting | bytes 29360128
  20.5 0.0 copy-start
  20.5 109.2 %shard_map.85 = bf16[512,7168]{1,0:T(8,128)(2,1)} custom-call(bf16[512,1024]{1,0:T(8,128)(2,1)} %bitcast.33, bf16[1024,7168]{1,0:T(8,128)(2,1)} %bitcast.31, bf16[32,7168]{1,0:T(8,128)(2,1)} %bitcast.41), custom_call_target="tpu_custom_call" | custom-call | flops 7516192768 | bytes 22020096 | tf_op jit(solution)/shard_map/pallas_call | solution.py:174
  129.7 0.0 copy-done
  129.8 0.0 copy-start.1
  129.8 13.4 %fusion.5 = (f32[1024]{0:T(1024)S(1)}, bf16[512,1024]{1,0:T(8,128)(2,1)S(1)}) fusion(bf16[512,7168]{1,0:T(8,128)(2,1)} %shard_map.85, bf16[1024,7168]{1,0:T(8,128)(2,1)} %bitcast.32, bf16[512,1024]{1,0:T(8,128)(2,1)S(1)} %bitcast.34), kind=kOutput, calls=%fused_computation.15 | convolution fusion | flops 7518288896 | bytes 24121344 | tf_op jit(solution)/shard_map/dot_general | solution.py:253
  143.1 0.6 broadcast_multiply_fusion
  143.7 0.1 copy.17
  143.8 0.0 copy-done.1
  143.8 6.1 %fusion = bf16[3584,1024]{0,1:T(8,128)(2,1)} fusion(bf16[512,1024]{1,0:T(8,128)(2,1)S(1)} %bitcast.39, bf16[512,3584]{1,0:T(8,128)(2,1)S(1)} %copy-done.1), kind=kOutput, calls=%fused_computation.4 | convolution fusion | flops 3765436416 | bytes 12058624 | tf_op jit(solution)/shard_map/dot_general | solution.py:261
  150.0 10.4 %copy.18 = bf16[3584,1024]{1,0:T(8,128)(2,1)} copy(bf16[3584,1024]{0,1:T(8,128)(2,1)} %fusion) | data formatting | bytes 14680064
  160.4 6.3 %fusion.2 = bf16[1024,1,3584]{2,0,1:T(8,128)(2,1)S(1)} fusion(bf16[512,1024]{1,0:T(8,128)(2,1)S(1)} %bitcast.35, bf16[512,7168]{1,0:T(8,128)(2,1)} %shard_map.85), kind=kOutput, calls=%fused_computation.6 | convolution fusion | flops 3765436416 | bytes 12058624 | tf_op jit(solution)/shard_map/dot_general | solution.py:241
  166.7 6.3 %fusion.1 = bf16[1024,1,3584]{2,0,1:T(8,128)(2,1)S(1)} fusion(bf16[512,1024]{1,0:T(8,128)(2,1)S(1)} %bitcast.36, bf16[512,7168]{1,0:T(8,128)(2,1)} %shard_map.85), kind=kOutput, calls=%fused_computation.5 | convolution fusion | flops 3765436416 | bytes 12058624 | tf_op jit(solution)/shard_map/dot_general | solution.py:241
  173.0 1.4 pad_maximum_fusion
  174.5 80.8 %copy.19 = bf16[1024,2,3584]{2,1,0:T(2,128)(2,1)} copy(bf16[1024,2,3584]{2,0,1:T(8,128)(2,1)S(1)} %pad_maximum_fusion) | data formatting | bytes 29360128
  (3 shorter events, 0.0 us)
Async XLA Ops:
  3.4 9.3 %slice-start = ((s8[14680064]{0:T(1024)(128)(4,1)}), s8[4194304]{0:T(1024)(128)(4,1)S(1)}, s32[]{:S(2)}) async-start(s8[14680064]{0:T(1024)(128)(4,1)} %bitcast.28), calls=%async_computation | async-start | bytes 8388608
  3.4 9.3 %slice-start.1 = ((s8[14680064]{0:T(1024)(128)(4,1)}), s8[4194304]{0:T(1024)(128)(4,1)S(1)}, s32[]{:S(2)}) async-start(s8[14680064]{0:T(1024)(128)(4,1)} %bitcast.28), calls=%async_computation.1 | async-start | bytes 8388608
  3.4 9.3 %slice-start.2 = ((s8[14680064]{0:T(1024)(128)(4,1)}), s8[4194304]{0:T(1024)(128)(4,1)S(1)}, s32[]{:S(2)}) async-start(s8[14680064]{0:T(1024)(128)(4,1)} %bitcast.28), calls=%async_computation.2 | async-start | bytes 8388608
  3.4 9.3 %slice-start.3 = ((s8[14680064]{0:T(1024)(128)(4,1)}), s8[2097152]{0:T(1024)(128)(4,1)S(1)}, s32[]{:S(2)}) async-start(s8[14680064]{0:T(1024)(128)(4,1)} %bitcast.28), calls=%async_computation.3 | async-start | bytes 4194304
  20.5 109.2 %copy-start = (bf16[4,2,2,32,1024]{4,3,0,1,2:T(8,128)(2,1)S(1)}, bf16[4,2,2,32,1024]{4,3,0,1,2:T(8,128)(2,1)}, u32[]{:S(2)}) copy-start(bf16[4,2,2,32,1024]{4,3,0,1,2:T(8,128)(2,1)} %copy.16) | copy-start | bytes 3145732
  129.8 14.1 %copy-start.1 = (bf16[512,3584]{1,0:T(8,128)(2,1)S(1)}, bf16[512,3584]{1,0:T(8,128)(2,1)}, u32[]{:S(2)}) copy-start(bf16[512,3584]{1,0:T(8,128)(2,1)} %param.6) | copy-start | bytes 11010052

commit v2 on v1

--- a/solution.py
+++ b/solution.py
@@ -11,12 +11,14 @@
 TILE = 128
 ZN, YN, CN = 4, 2, 2
 PEERS = 5
+STRIP = 256
 CORE, YRS, ZRS, ZAG, YAG, CAG, KINDS = 0, 1, 2, 5, 8, 9, 10
 LAG = (1, 3, 5, 7, 9, 10)
 
 
 def exchange_kernel(
-    chunks, feats, w_hbm, tgt, out, wbuf, part, r_core, r_y, r_z, w_sem, send, recv
+    chunks, scale, feats, w_hbm, tgt, gfeat, gdec, out, wbuf, part, r_core, r_y, r_z, feats_t, held,
+    w_sem, send, recv, out_sem,
 ):
     me = lax.axis_index("layer")
     z, y, c = me // 4, (me // 2) % 2, me % 2
@@ -56,6 +58,11 @@
     def load(k):
         return pltpu.make_async_copy(w_hbm.at[:, at(k)], wbuf.at[:, at(k)], w_sem.at[k])
 
+    def store(k):
+        per = gdec.shape[3] // width
+        dst = gdec.at[:, k // per, :, pl.ds(pl.multiple_of((k % per) * width, 128), width)]
+        return pltpu.make_async_copy(held.at[k % 2], dst, out_sem.at[k % 2])
+
     def core_copy(k):
         return copy(part.at[far_half, at(k)], r_core.at[:, at(k)], CORE, k, core_peer)
 
@@ -96,6 +103,8 @@
     def _(k):
         load(k).start()
 
+    feats_t[...] = feats[...].T
+    gfeat[...] = jnp.zeros_like(gfeat)
     pl.semaphore_wait(barrier, PEERS)
 
     @pl.loop(0, chunks + LAG[-1])
@@ -150,10 +159,35 @@
         def after_cag(k):
             core_take(k).wait_recv()
 
+            @pl.when(k >= 2)
+            def _():
+                store(k - 2).wait()
+
+            @pl.loop(0, feats.shape[1] // STRIP)
+            def _(j):
+                strip = pl.ds(pl.multiple_of(j * STRIP, STRIP), STRIP)
+                grad = jnp.dot(
+                    feats_t[strip, :], out[:, at(k)], preferred_element_type=jnp.float32
+                )
+                held[k % 2, pl.ds(j * (STRIP // 8), STRIP // 8)] = (
+                    (grad * scale).reshape(STRIP // 8, 8, width).astype(jnp.bfloat16)
+                )
+                gfeat[:, strip] += lax.dot_general(
+                    out[:, at(k)],
+                    wbuf[strip, at(k)],
+                    (((1,), (1,)), ((), ())),
+                    preferred_element_type=jnp.float32,
+                )
+
+            store(k).start()
+
         for lag, body in zip(
             LAG, (after_core, after_y, after_z, after_zag, after_yag, after_cag)
         ):
             stage(lag, body)
+
+    for k in (chunks - 2, chunks - 1):
+        store(k).wait()
 
     @pl.loop(0, chunks)
     def _(k):
@@ -166,39 +200,71 @@
         core_send(k).wait_send()
 
 
-def exchange(feats, w_flat, tgt):
+def exchange(feats, w_flat, tgt, targets, scale):
     tokens, depth = feats.shape
     columns = w_flat.shape[1]
     rows = tgt.shape[0]
-    chunks = 8
+    chunks = 14
     return pl.pallas_call(
-        functools.partial(exchange_kernel, chunks),
-        out_shape=jax.ShapeDtypeStruct((tokens, columns), jnp.bfloat16),
+        functools.partial(exchange_kernel, chunks, scale),
+        out_shape=(
+            jax.ShapeDtypeStruct((tokens, depth), jnp.float32),
+            jax.ShapeDtypeStruct((depth // 8, targets, 8, columns // targets), jnp.bfloat16),
+        ),
         in_specs=[
             pl.BlockSpec(memory_space=pltpu.VMEM),
             pl.BlockSpec(memory_space=pl.ANY),
             pl.BlockSpec(memory_space=pltpu.VMEM),
         ],
-        out_specs=pl.BlockSpec(memory_space=pltpu.VMEM),
+        out_specs=(pl.BlockSpec(memory_space=pltpu.VMEM), pl.BlockSpec(memory_space=pl.ANY)),
         scratch_shapes=[
+            pltpu.VMEM((tokens, columns), jnp.bfloat16),
             pltpu.VMEM((depth, columns), jnp.bfloat16),
             pltpu.VMEM((tokens, columns), jnp.bfloat16),
             pltpu.VMEM((tokens // CN, columns), jnp.bfloat16),
             pltpu.VMEM((tokens // CN // YN, columns), jnp.bfloat16),
             pltpu.VMEM((ZN - 1, rows, columns), jnp.bfloat16),
+            pltpu.VMEM((depth, tokens), jnp.bfloat16),
+            pltpu.VMEM((2, depth // 8, 8, columns // chunks), jnp.bfloat16),
             pltpu.SemaphoreType.DMA((chunks,)),
             pltpu.SemaphoreType.DMA((KINDS, chunks)),
             pltpu.SemaphoreType.DMA((KINDS, chunks)),
+            pltpu.SemaphoreType.DMA((2,)),
         ],
         compiler_params=pltpu.CompilerParams(
-            collective_id=0, has_side_effects=True, vmem_limit_bytes=56 * 2**20
+            collective_id=0, has_side_effects=True, vmem_limit_bytes=58 * 2**20
         ),
         cost_estimate=pl.CostEstimate(
-            flops=2 * tokens * depth * columns,
-            bytes_accessed=2 * (depth + tokens) * columns,
+            flops=6 * tokens * depth * columns,
+            bytes_accessed=2 * (2 * depth + tokens) * columns,
             transcendentals=0,
         ),
     )(feats, w_flat, tgt)
+
+
+def enc_grad(inputs, gfeat, scale):
+    tokens, d = inputs.shape
+    f = gfeat.shape[1]
+
+    def body(x, g, o):
+        o[...] = (
+            lax.dot_general(
+                x[...], g[...], (((0,), (0,)), ((), ())), preferred_element_type=jnp.float32
+            )
+            * scale
+        ).astype(jnp.bfloat16)
+
+    return pl.pallas_call(
+        body,
+        grid=(d // 512,),
+        out_shape=jax.ShapeDtypeStruct((d, f), jnp.bfloat16),
+        in_specs=[
+            pl.BlockSpec((tokens, 512), lambda i: (0, i)),
+            pl.BlockSpec((tokens, f), lambda i: (0, 0)),
+        ],
+        out_specs=pl.BlockSpec((512, f), lambda i: (i, 0)),
+        compiler_params=pltpu.CompilerParams(vmem_limit_bytes=32 * 2**20),
+    )(inputs, gfeat)
 
 
 def by_owner(a, back=False):
@@ -225,7 +291,8 @@
     tgt = targets.reshape(tok_rows, n_targets * width)
     if own:
         feats = by_owner(feats)
-        err_all = exchange(feats, w_flat, tgt)
+        gfeat, gdec = exchange(feats, w_flat, tgt, n_targets, scale)
+        grad_dec = gdec.transpose(0, 2, 1, 3).reshape(w_dec.shape)
     else:
         recon = lax.psum_scatter(
             jnp.dot(feats, w_flat, preferred_element_type=jnp.float32),
@@ -235,37 +302,21 @@
         )
         err = (recon - tgt.astype(jnp.float32)).astype(jnp.bfloat16)
         err_all = lax.all_gather(err, "layer", axis=0, tiled=True)
-    grad_dec = jnp.stack(
-        [
-            (
-                lax.dot_general(
-                    feats,
-                    err_all[:, t * width : (t + 1) * width],
-                    (((0,), (0,)), ((), ())),
-                    preferred_element_type=jnp.float32,
-                )
-                * scale
-            ).astype(jnp.bfloat16)
-            for t in range(n_targets)
-        ],
-        axis=1,
-    )
-    gfeat = lax.dot_general(
-        err_all, w_flat, (((1,), (1,)), ((), ())), preferred_element_type=jnp.float32
-    ) * (feats > 0)
+        grad_dec = (
+            lax.dot_general(
+                feats, err_all, (((0,), (0,)), ((), ())), preferred_element_type=jnp.float32
+            )
+            * scale
+        ).astype(jnp.bfloat16).reshape(w_dec.shape)
+        gfeat = lax.dot_general(
+            err_all, w_flat, (((1,), (1,)), ((), ())), preferred_element_type=jnp.float32
+        )
+    gfeat = gfeat * (feats > 0)
     grad_bias = jnp.sum(gfeat, axis=0) * scale
     gfeat_b = gfeat.astype(jnp.bfloat16)
     if own:
         gfeat_b = by_owner(gfeat_b, back=True)
-    grad_enc = (
-        lax.dot_general(
-            inputs,
-            gfeat_b,
-            (((0,), (0,)), ((), ())),
-            preferred_element_type=jnp.float32,
-        )
-        * scale
-    ).astype(jnp.bfloat16)
+    grad_enc = enc_grad(inputs, gfeat_b, scale)
     return (grad_enc, grad_bias, grad_dec)
 
 

time: 258 us -> 225 us (0.87)
  matrix products: 40.4 us -> 8.23 us
  Pallas kernels: 109 us -> 114 us
    dot_general x4 -> x0, matrix products: 32.1 us -> none  [the longest x1 13.4 us: local(): lax.dot_general(err_all, w_flat, (((1,), (1,)), ((), ())), preferred_elem...]
    unnamed x16 -> x17, local copies, waits for them, and re-layouts: 101 us -> 90.9 us
    reshape x0 -> x1, local copies, waits for them, and re-layouts: none -> 7.42 us  [local(): grad_dec = gdec.transpose(0, 2, 1, 3).reshape(w_dec.shape)]
    pallas_call x1 -> x2, Pallas kernels: 109 us -> 114 us  [the longest x1 107 us: exchange(): pl.pallas_call(functools.partial(exchange_kernel, chunks, scale), out_sha...]
where the time goes in v2:
time: 225 us
  Pallas kernels  114 us (51%)
  local copies, waits for them, and re-layouts  99.6 us (44%)
  matrix products  8.23 us (4%)
  other arithmetic  2.31 us (1%)
    pallas_call x1, Pallas kernels, exchange(): pl.pallas_call(functools.partial(exchange_kernel, chunks, scale), out_sha...  107 us
    unnamed x17, local copies, waits for them, and re-layouts  90.9 us
    dot_general x1, matrix products, local(): pre = jnp.dot(inputs, w_enc, preferred_element_type=jnp.float32) + b_enc  8.23 us
    reshape x1, local copies, waits for them, and re-layouts, local(): grad_dec = gdec.transpose(0, 2, 1, 3).reshape(w_dec.shape)  7.42 us
    pallas_call x1, Pallas kernels, enc_grad(): pl.pallas_call(body, grid=(d // 512,), out_shape=jax.ShapeDtypeStruct((d,...  7 us

profile of v2, /device:TPU:0, one launch (start us, length us, event | category | flops | bytes accessed | tf_op | source)
XLA Modules:
  0.0 224.8 jit_solution(13789673501309827070)
XLA Ops:
  0.6 0.8 compare_reduce_fusion
  1.5 0.1 broadcast_bitcast_fusion
  1.6 1.8 copy.20
  3.4 0.0 slice-start
  3.4 0.0 slice-start.1
  3.4 0.0 slice-start.2
  3.4 0.0 slice-start.3
  3.4 8.2 %multiply_convert_fusion = bf16[512,1024]{1,0:T(8,128)(2,1)S(1)} fusion(bf16[512,3584]{1,0:T(8,128)(2,1)} %x.1, bf16[3584,1024]{1,0:T(8,128)(2,1)} %param.8, f32[1024]{0:T(1024)S(1)} %broadcast_bitcast_fusion, f32[1024]{0:T(1024)} %param.9), kind=kOutput, calls=%fused_computation.1 | convolution fusion | flops 3760193536 | bytes 12066816 | tf_op jit(solution)/shard_map/dot_general | solution.py:286
  11.7 1.1 copy.15
  12.7 0.0 slice-done
  12.7 0.0 slice-done.1
  12.7 0.0 slice-done.2
  12.7 0.0 slice-done.3
  12.8 7.6 %copy.19 = bf16[128,8,2,3584]{3,1,2,0:T(8,128)(2,1)} copy(bf16[128,8,2,3584]{3,2,1,0:T(2,128)(2,1)S(1)} %bitcast.26) | data formatting | bytes 29360128
  20.4 106.9 %shard_map.85 = (f32[512,1024]{1,0:T(8,128)}, bf16[128,2,8,3584]{3,2,1,0:T(8,128)(2,1)}) custom-call(bf16[512,1024]{1,0:T(8,128)(2,1)} %bitcast.28, bf16[1024,7168]{1,0:T(8,128)(2,1)} %bitcast.27, bf16[32,7168]{1,0:T(8,128)(2,1)} %bitcast.32), custom_call_target="tpu_custom_call" | custom-call | flops 22548578304 | bytes 36700160 | tf_op jit(solution)/shard_map/pallas_call | solution.py:208
  127.3 7.4 %copy_bitcast_fusion = bf16[1024,2,3584]{2,0,1:T(8,128)(2,1)S(1)} fusion(bf16[128,2,8,3584]{3,2,1,0:T(8,128)(2,1)} %get-tuple-element.6), kind=kLoop, calls=%fused_computation | loop fusion | bytes 29360128 | tf_op jit(solution)/shard_map/reshape | solution.py:295
  134.7 0.0 copy-start.1
  134.7 0.0 copy-start.2
  134.8 80.6 %copy.18 = bf16[1024,2,3584]{2,1,0:T(2,128)(2,1)} copy(bf16[1024,2,3584]{2,0,1:T(8,128)(2,1)S(1)} %copy_bitcast_fusion) | data formatting | bytes 29360128
  215.4 0.0 copy-done.1
  215.4 0.0 copy-done.2
  215.4 0.4 fusion
  215.8 0.0 copy-start
  215.8 0.5 fusion.1
  216.2 0.1 copy.16
  216.3 0.6 broadcast_multiply_fusion
  216.9 0.9 copy-done
  217.8 7.0 %shard_map.86 = bf16[3584,1024]{1,0:T(8,128)(2,1)} custom-call(bf16[512,3584]{1,0:T(8,128)(2,1)S(1)} %copy-done, bf16[512,1024]{1,0:T(8,128)(2,1)S(1)} %bitcast.23), custom_call_target="tpu_custom_call" | custom-call | tf_op jit(solution)/shard_map/pallas_call | solution.py:257
  (3 shorter events, 0.0 us)
Async XLA Ops:
  3.4 9.3 %slice-start = ((s8[14680064]{0:T(1024)(128)(4,1)}), s8[4194304]{0:T(1024)(128)(4,1)S(1)}, s32[]{:S(2)}) async-start(s8[14680064]{0:T(1024)(128)(4,1)} %bitcast.24), calls=%async_computation | async-start | bytes 8388608
  3.4 9.3 %slice-start.1 = ((s8[14680064]{0:T(1024)(128)(4,1)}), s8[4194304]{0:T(1024)(128)(4,1)S(1)}, s32[]{:S(2)}) async-start(s8[14680064]{0:T(1024)(128)(4,1)} %bitcast.24), calls=%async_computation.1 | async-start | bytes 8388608
  3.4 9.3 %slice-start.2 = ((s8[14680064]{0:T(1024)(128)(4,1)}), s8[4194304]{0:T(1024)(128)(4,1)S(1)}, s32[]{:S(2)}) async-start(s8[14680064]{0:T(1024)(128)(4,1)} %bitcast.24), calls=%async_computation.2 | async-start | bytes 8388608
  3.4 9.3 %slice-start.3 = ((s8[14680064]{0:T(1024)(128)(4,1)}), s8[2097152]{0:T(1024)(128)(4,1)S(1)}, s32[]{:S(2)}) async-start(s8[14680064]{0:T(1024)(128)(4,1)} %bitcast.24), calls=%async_computation.3 | async-start | bytes 4194304
  134.7 80.6 %copy-start.1 = (bf16[4,2,2,32,1024]{4,3,0,1,2:T(8,128)(2,1)S(1)}, bf16[4,2,2,32,1024]{4,3,0,1,2:T(8,128)(2,1)}, u32[]{:S(2)}) copy-start(bf16[4,2,2,32,1024]{4,3,0,1,2:T(8,128)(2,1)} %copy.15) | copy-start | bytes 3145732
  134.7 80.6 %copy-start.2 = (f32[512,1024]{1,0:T(8,128)S(1)}, f32[512,1024]{1,0:T(8,128)}, u32[]{:S(2)}) copy-start(f32[512,1024]{1,0:T(8,128)} %get-tuple-element.5) | copy-start | bytes 6291460
  215.8 2.0 copy-start

commit v3 on v2

--- a/solution.py
+++ b/solution.py
@@ -59,9 +59,7 @@
         return pltpu.make_async_copy(w_hbm.at[:, at(k)], wbuf.at[:, at(k)], w_sem.at[k])
 
     def store(k):
-        per = gdec.shape[3] // width
-        dst = gdec.at[:, k // per, :, pl.ds(pl.multiple_of((k % per) * width, 128), width)]
-        return pltpu.make_async_copy(held.at[k % 2], dst, out_sem.at[k % 2])
+        return pltpu.make_async_copy(held.at[k % 2], gdec.at[:, at(k)], out_sem.at[k % 2])
 
     def core_copy(k):
         return copy(part.at[far_half, at(k)], r_core.at[:, at(k)], CORE, k, core_peer)
@@ -169,9 +167,7 @@
                 grad = jnp.dot(
                     feats_t[strip, :], out[:, at(k)], preferred_element_type=jnp.float32
                 )
-                held[k % 2, pl.ds(j * (STRIP // 8), STRIP // 8)] = (
-                    (grad * scale).reshape(STRIP // 8, 8, width).astype(jnp.bfloat16)
-                )
+                held[k % 2, strip, :] = (grad * scale).astype(jnp.bfloat16)
                 gfeat[:, strip] += lax.dot_general(
                     out[:, at(k)],
                     wbuf[strip, at(k)],
@@ -200,7 +196,7 @@
         core_send(k).wait_send()
 
 
-def exchange(feats, w_flat, tgt, targets, scale):
+def exchange(feats, w_flat, tgt, scale):
     tokens, depth = feats.shape
     columns = w_flat.shape[1]
     rows = tgt.shape[0]
@@ -209,7 +205,7 @@
         functools.partial(exchange_kernel, chunks, scale),
         out_shape=(
             jax.ShapeDtypeStruct((tokens, depth), jnp.float32),
-            jax.ShapeDtypeStruct((depth // 8, targets, 8, columns // targets), jnp.bfloat16),
+            jax.ShapeDtypeStruct((depth, columns), jnp.bfloat16),
         ),
         in_specs=[
             pl.BlockSpec(memory_space=pltpu.VMEM),
@@ -225,7 +221,7 @@
             pltpu.VMEM((tokens // CN // YN, columns), jnp.bfloat16),
             pltpu.VMEM((ZN - 1, rows, columns), jnp.bfloat16),
             pltpu.VMEM((depth, tokens), jnp.bfloat16),
-            pltpu.VMEM((2, depth // 8, 8, columns // chunks), jnp.bfloat16),
+            pltpu.VMEM((2, depth, columns // chunks), jnp.bfloat16),
             pltpu.SemaphoreType.DMA((chunks,)),
             pltpu.SemaphoreType.DMA((KINDS, chunks)),
             pltpu.SemaphoreType.DMA((KINDS, chunks)),
@@ -265,6 +261,40 @@
         out_specs=pl.BlockSpec((512, f), lambda i: (i, 0)),
         compiler_params=pltpu.CompilerParams(vmem_limit_bytes=32 * 2**20),
     )(inputs, gfeat)
+
+
+def by_target(flat, tile_on, targets):
+    features, columns = flat.shape
+    width = columns // targets
+    block = 512
+    steps = width // block
+
+    def body(on, *refs):
+        o = refs[-1]
+
+        @pl.when(on[pl.program_id(0)] != 0)
+        def _():
+            for t in range(targets):
+                o[:, t, :] = refs[t][...]
+
+        @pl.when(on[pl.program_id(0)] == 0)
+        def _():
+            o[...] = jnp.zeros_like(o)
+
+    return pl.pallas_call(
+        body,
+        out_shape=jax.ShapeDtypeStruct((features, targets, width), flat.dtype),
+        grid_spec=pltpu.PrefetchScalarGridSpec(
+            num_scalar_prefetch=1,
+            grid=(features // TILE, steps),
+            in_specs=[
+                pl.BlockSpec((TILE, block), lambda i, j, on, t=t: (i, t * steps + j))
+                for t in range(targets)
+            ],
+            out_specs=pl.BlockSpec((TILE, targets, block), lambda i, j, on: (i, 0, j)),
+        ),
+        compiler_params=pltpu.CompilerParams(vmem_limit_bytes=32 * 2**20),
+    )(tile_on, *[flat] * targets)
 
 
 def by_owner(a, back=False):
@@ -291,8 +321,8 @@
     tgt = targets.reshape(tok_rows, n_targets * width)
     if own:
         feats = by_owner(feats)
-        gfeat, gdec = exchange(feats, w_flat, tgt, n_targets, scale)
-        grad_dec = gdec.transpose(0, 2, 1, 3).reshape(w_dec.shape)
+        gfeat, gdec = exchange(feats, w_flat, tgt, scale)
+        grad_dec = by_target(gdec, tile_on.astype(jnp.int32), n_targets)
     else:
         recon = lax.psum_scatter(
             jnp.dot(feats, w_flat, preferred_element_type=jnp.float32),

time: 225 us -> 167 us (0.74)
  local copies, waits for them, and re-layouts: 99.6 us -> 16.7 us
  Pallas kernels: 114 us -> 137 us
    unnamed x17 -> x18, local copies, waits for them, and re-layouts: 90.9 us -> 15.5 us
    pallas_call x0 -> x1, Pallas kernels: none -> 22.9 us  [by_target(): pl.pallas_call(body, out_shape=jax.ShapeDtypeStruct((features, targets, w...]
    reshape x1 -> x0, local copies, waits for them, and re-layouts: 7.42 us -> none  [local(): grad_dec = gdec.transpose(0, 2, 1, 3).reshape(w_dec.shape)]
where the time goes in v3:
time: 167 us; the launch traced here: 165 us
  Pallas kernels  137 us (82%)
  local copies, waits for them, and re-layouts  16.7 us (10%)
  matrix products  8.23 us (5%)
  other arithmetic  2.31 us (1%)
    pallas_call x1, Pallas kernels, exchange(): pl.pallas_call(functools.partial(exchange_kernel, chunks, scale), out_sha...  107 us
    pallas_call x1, Pallas kernels, by_target(): pl.pallas_call(body, out_shape=jax.ShapeDtypeStruct((features, targets, w...  22.9 us
    unnamed x18, local copies, waits for them, and re-layouts  15.5 us
    dot_general x1, matrix products, local(): pre = jnp.dot(inputs, w_enc, preferred_element_type=jnp.float32) + b_enc  8.23 us
    pallas_call x1, Pallas kernels, enc_grad(): pl.pallas_call(body, grid=(d // 512,), out_shape=jax.ShapeDtypeStruct((d,...  6.99 us

profile of v3, /device:TPU:0, one launch (start us, length us, event | category | flops | bytes accessed | tf_op | source)
XLA Modules:
  0.0 164.6 jit_solution(17055096663141744788)
XLA Ops:
  0.6 0.8 compare_reduce_fusion
  1.5 0.1 broadcast_bitcast_fusion
  1.6 1.8 %copy.14 = bf16[4,8,2,3584]{3,1,2,0:T(8,128)(2,1)} copy(bf16[4,8,2,3584]{3,2,1,0:T(2,128)(2,1)} %bitcast.26) | data formatting | bytes 917504
  3.4 0.0 slice-start
  3.4 0.0 slice-start.1
  3.4 0.0 slice-start.2
  3.4 0.0 slice-start.3
  3.4 8.2 %multiply_convert_fusion = bf16[512,1024]{1,0:T(8,128)(2,1)S(1)} fusion(bf16[512,3584]{1,0:T(8,128)(2,1)} %x.1, bf16[3584,1024]{1,0:T(8,128)(2,1)} %param.8, f32[1024]{0:T(1024)S(1)} %broadcast_bitcast_fusion, f32[1024]{0:T(1024)} %param.9), kind=kOutput, calls=%fused_computation | convolution fusion | flops 3760193536 | bytes 12066816 | tf_op jit(solution)/shard_map/dot_general | solution.py:316
  11.7 1.1 copy.11
  12.7 0.0 slice-done
  12.7 0.0 slice-done.1
  12.7 0.0 slice-done.2
  12.7 0.0 slice-done.3
  12.7 7.6 %copy.13 = bf16[128,8,2,3584]{3,1,2,0:T(8,128)(2,1)} copy(bf16[128,8,2,3584]{3,2,1,0:T(2,128)(2,1)S(1)} %bitcast.21) | data formatting | bytes 29360128
  20.3 106.8 %shard_map.85 = (f32[512,1024]{1,0:T(8,128)}, bf16[1024,7168]{1,0:T(8,128)(2,1)}) custom-call(bf16[512,1024]{1,0:T(8,128)(2,1)} %bitcast.23, bf16[1024,7168]{1,0:T(8,128)(2,1)} %bitcast.22, bf16[32,7168]{1,0:T(8,128)(2,1)} %bitcast.27), custom_call_target="tpu_custom_call" | custom-call | flops 22548578304 | bytes 36700160 | tf_op jit(solution)/shard_map/pallas_call | solution.py:204
  127.1 0.0 copy-start
  127.1 5.2 %copy-done = bf16[1024,7168]{1,0:T(8,128)(2,1)S(1)} copy-done((bf16[1024,7168]{1,0:T(8,128)(2,1)S(1)}, bf16[1024,7168]{1,0:T(8,128)(2,1)}, u32[]{:S(2)}) %copy-start) | copy-done | bytes 14680088
  132.3 0.0 copy-start.2
  132.3 0.0 copy-start.3
  132.3 22.9 %shard_map.87 = bf16[1024,2,3584]{2,1,0:T(2,128)(2,1)} custom-call(s32[8]{0:T(128)S(1)} %get-tuple-element.7.on, bf16[1024,7168]{1,0:T(8,128)(2,1)S(1)} %copy-done, bf16[1024,7168]{1,0:T(8,128)(2,1)S(1)} %copy-done), custom_call_target="tpu_custom_call" | custom-call | tf_op jit(solution)/shard_map/pallas_call | solution.py:284
  155.2 0.0 copy-done.2
  155.2 0.0 copy-done.3
  155.2 0.4 fusion
  155.6 0.0 copy-start.1
  155.6 0.5 fusion.1
  156.1 0.1 copy.12
  156.2 0.6 broadcast_multiply_fusion
  156.8 0.9 copy-done.1
  157.6 7.0 %shard_map.86 = bf16[3584,1024]{1,0:T(8,128)(2,1)} custom-call(bf16[512,3584]{1,0:T(8,128)(2,1)S(1)} %copy-done.1, bf16[512,1024]{1,0:T(8,128)(2,1)S(1)} %bitcast.18), custom_call_target="tpu_custom_call" | custom-call | tf_op jit(solution)/shard_map/pallas_call | solution.py:253
  (3 shorter events, 0.0 us)
Async XLA Ops:
  3.4 9.3 %slice-start = ((s8[14680064]{0:T(1024)(128)(4,1)}), s8[4194304]{0:T(1024)(128)(4,1)S(1)}, s32[]{:S(2)}) async-start(s8[14680064]{0:T(1024)(128)(4,1)} %bitcast.19), calls=%async_computation | async-start | bytes 8388608
  3.4 9.3 %slice-start.1 = ((s8[14680064]{0:T(1024)(128)(4,1)}), s8[4194304]{0:T(1024)(128)(4,1)S(1)}, s32[]{:S(2)}) async-start(s8[14680064]{0:T(1024)(128)(4,1)} %bitcast.19), calls=%async_computation.1 | async-start | bytes 8388608
  3.4 9.3 %slice-start.2 = ((s8[14680064]{0:T(1024)(128)(4,1)}), s8[4194304]{0:T(1024)(128)(4,1)S(1)}, s32[]{:S(2)}) async-start(s8[14680064]{0:T(1024)(128)(4,1)} %bitcast.19), calls=%async_computation.2 | async-start | bytes 8388608
  3.4 9.3 %slice-start.3 = ((s8[14680064]{0:T(1024)(128)(4,1)}), s8[2097152]{0:T(1024)(128)(4,1)S(1)}, s32[]{:S(2)}) async-start(s8[14680064]{0:T(1024)(128)(4,1)} %bitcast.19), calls=%async_computation.3 | async-start | bytes 4194304
  127.1 5.2 %copy-start = (bf16[1024,7168]{1,0:T(8,128)(2,1)S(1)}, bf16[1024,7168]{1,0:T(8,128)(2,1)}, u32[]{:S(2)}) copy-start(bf16[1024,7168]{1,0:T(8,128)(2,1)} %get-tuple-element.6.refs_0_.refs_1_) | copy-start | bytes 44040196
  132.3 22.9 %copy-start.2 = (bf16[4,2,2,32,1024]{4,3,0,1,2:T(8,128)(2,1)S(1)}, bf16[4,2,2,32,1024]{4,3,0,1,2:T(8,128)(2,1)}, u32[]{:S(2)}) copy-start(bf16[4,2,2,32,1024]{4,3,0,1,2:T(8,128)(2,1)} %copy.11) | copy-start | bytes 3145732
  132.3 22.9 %copy-start.3 = (f32[512,1024]{1,0:T(8,128)S(1)}, f32[512,1024]{1,0:T(8,128)}, u32[]{:S(2)}) copy-start(f32[512,1024]{1,0:T(8,128)} %get-tuple-element.5) | copy-start | bytes 6291460
  155.6 2.0 %copy-start.1 = (bf16[512,3584]{1,0:T(8,128)(2,1)S(1)}, bf16[512,3584]{1,0:T(8,128)(2,1)}, u32[]{:S(2)}) copy-start(bf16[512,3584]{1,0:T(8,128)(2,1)} %x.1) | copy-start | bytes 11010052

commit v4 on v3

--- a/solution.py
+++ b/solution.py
@@ -266,7 +266,7 @@
 def by_target(flat, tile_on, targets):
     features, columns = flat.shape
     width = columns // targets
-    block = 512
+    block = 896
     steps = width // block
 
     def body(on, *refs):
@@ -293,7 +293,7 @@
             ],
             out_specs=pl.BlockSpec((TILE, targets, block), lambda i, j, on: (i, 0, j)),
         ),
-        compiler_params=pltpu.CompilerParams(vmem_limit_bytes=32 * 2**20),
+        compiler_params=pltpu.CompilerParams(vmem_limit_bytes=58 * 2**20),
     )(tile_on, *[flat] * targets)
 
 

time: 167 us -> 163 us (0.976)
  local copies, waits for them, and re-layouts: 16.7 us -> 11.5 us
    unnamed x18 -> x16, local copies, waits for them, and re-layouts: 15.5 us -> 10.3 us
where the time goes in v4:
time: 163 us; the launch traced here: 161 us
  Pallas kernels  137 us (84%)
  local copies, waits for them, and re-layouts  11.5 us (7%)
  matrix products  8.23 us (5%)
  other arithmetic  2.82 us (2%)
    pallas_call x1, Pallas kernels, exchange(): pl.pallas_call(functools.partial(exchange_kernel, chunks, scale), out_sha...  107 us
    pallas_call x1, Pallas kernels, by_target(): pl.pallas_call(body, out_shape=jax.ShapeDtypeStruct((features, targets, w...  23.4 us
    unnamed x16, local copies, waits for them, and re-layouts  10.3 us
    dot_general x1, matrix products, local(): pre = jnp.dot(inputs, w_enc, preferred_element_type=jnp.float32) + b_enc  8.23 us
    pallas_call x1, Pallas kernels, enc_grad(): pl.pallas_call(body, grid=(d // 512,), out_shape=jax.ShapeDtypeStruct((d,...  6.99 us

profile of v4, /device:TPU:0, one launch (start us, length us, event | category | flops | bytes accessed | tf_op | source)
XLA Modules:
  0.0 160.6 jit_solution(12556270833042888179)
XLA Ops:
  0.6 0.8 compare_reduce_fusion
  1.5 0.5 fusion.2
  2.0 0.1 broadcast_bitcast_fusion
  2.1 1.8 %copy.14 = bf16[4,8,2,3584]{3,1,2,0:T(8,128)(2,1)} copy(bf16[4,8,2,3584]{3,2,1,0:T(2,128)(2,1)} %bitcast.26) | data formatting | bytes 917504
  3.9 0.0 slice-start
  3.9 0.0 slice-start.1
  3.9 0.0 slice-start.2
  3.9 0.0 slice-start.3
  3.9 8.2 %multiply_convert_fusion = bf16[512,1024]{1,0:T(8,128)(2,1)S(1)} fusion(bf16[512,3584]{1,0:T(8,128)(2,1)} %x.1, bf16[3584,1024]{1,0:T(8,128)(2,1)} %param.8, f32[1024]{0:T(1024)S(1)} %broadcast_bitcast_fusion, f32[1024]{0:T(1024)} %param.9), kind=kOutput, calls=%fused_computation | convolution fusion | flops 3760193536 | bytes 12066816 | tf_op jit(solution)/shard_map/dot_general | solution.py:316
  12.2 1.1 copy.11
  13.2 0.0 slice-done
  13.2 0.0 slice-done.1
  13.2 0.0 slice-done.2
  13.2 0.0 slice-done.3
  13.2 7.6 %copy.13 = bf16[128,8,2,3584]{3,1,2,0:T(8,128)(2,1)} copy(bf16[128,8,2,3584]{3,2,1,0:T(2,128)(2,1)S(1)} %bitcast.21) | data formatting | bytes 29360128
  20.8 106.9 %shard_map.85 = (f32[512,1024]{1,0:T(8,128)}, bf16[1024,7168]{1,0:T(8,128)(2,1)}) custom-call(bf16[512,1024]{1,0:T(8,128)(2,1)} %bitcast.23, bf16[1024,7168]{1,0:T(8,128)(2,1)} %bitcast.22, bf16[32,7168]{1,0:T(8,128)(2,1)} %bitcast.27), custom_call_target="tpu_custom_call" | custom-call | flops 22548578304 | bytes 36700160 | tf_op jit(solution)/shard_map/pallas_call | solution.py:204
  127.7 0.0 copy-start.1
  127.7 0.0 copy-start.2
  127.7 23.4 %shard_map.87 = bf16[1024,2,3584]{2,1,0:T(2,128)(2,1)} custom-call(s32[8]{0:T(128)} %get-tuple-element.7.on, bf16[1024,7168]{1,0:T(8,128)(2,1)} %get-tuple-element.6.refs_0_.refs_1_, bf16[1024,7168]{1,0:T(8,128)(2,1)} %get-tuple-element.6.refs_0_.refs_1_), custom_call_target="tpu_custom_call" | custom-call | tf_op jit(solution)/shard_map/pallas_call | solution.py:284
  151.2 0.0 copy-done.1
  151.2 0.0 copy-done.2
  151.2 0.4 fusion
  151.6 0.0 copy-start
  151.6 0.5 fusion.1
  152.0 0.1 copy.12
  152.1 0.6 broadcast_multiply_fusion
  152.7 0.9 copy-done
  153.6 7.0 %shard_map.86 = bf16[3584,1024]{1,0:T(8,128)(2,1)} custom-call(bf16[512,3584]{1,0:T(8,128)(2,1)S(1)} %copy-done, bf16[512,1024]{1,0:T(8,128)(2,1)S(1)} %bitcast.18), custom_call_target="tpu_custom_call" | custom-call | tf_op jit(solution)/shard_map/pallas_call | solution.py:253
  (2 shorter events, 0.0 us)
Async XLA Ops:
  3.9 9.3 %slice-start = ((s8[14680064]{0:T(1024)(128)(4,1)}), s8[4194304]{0:T(1024)(128)(4,1)S(1)}, s32[]{:S(2)}) async-start(s8[14680064]{0:T(1024)(128)(4,1)} %bitcast.19), calls=%async_computation | async-start | bytes 8388608
  3.9 9.3 %slice-start.1 = ((s8[14680064]{0:T(1024)(128)(4,1)}), s8[4194304]{0:T(1024)(128)(4,1)S(1)}, s32[]{:S(2)}) async-start(s8[14680064]{0:T(1024)(128)(4,1)} %bitcast.19), calls=%async_computation.1 | async-start | bytes 8388608
  3.9 9.3 %slice-start.2 = ((s8[14680064]{0:T(1024)(128)(4,1)}), s8[4194304]{0:T(1024)(128)(4,1)S(1)}, s32[]{:S(2)}) async-start(s8[14680064]{0:T(1024)(128)(4,1)} %bitcast.19), calls=%async_computation.2 | async-start | bytes 8388608
  3.9 9.3 %slice-start.3 = ((s8[14680064]{0:T(1024)(128)(4,1)}), s8[2097152]{0:T(1024)(128)(4,1)S(1)}, s32[]{:S(2)}) async-start(s8[14680064]{0:T(1024)(128)(4,1)} %bitcast.19), calls=%async_computation.3 | async-start | bytes 4194304
  127.7 23.5 %copy-start.1 = (bf16[4,2,2,32,1024]{4,3,0,1,2:T(8,128)(2,1)S(1)}, bf16[4,2,2,32,1024]{4,3,0,1,2:T(8,128)(2,1)}, u32[]{:S(2)}) copy-start(bf16[4,2,2,32,1024]{4,3,0,1,2:T(8,128)(2,1)} %copy.11) | copy-start | bytes 3145732
  127.7 23.5 %copy-start.2 = (f32[512,1024]{1,0:T(8,128)S(1)}, f32[512,1024]{1,0:T(8,128)}, u32[]{:S(2)}) copy-start(f32[512,1024]{1,0:T(8,128)} %get-tuple-element.5) | copy-start | bytes 6291460
  151.6 2.0 %copy-start = (bf16[512,3584]{1,0:T(8,128)(2,1)S(1)}, bf16[512,3584]{1,0:T(8,128)(2,1)}, u32[]{:S(2)}) copy-start(bf16[512,3584]{1,0:T(8,128)(2,1)} %x.1) | copy-start | bytes 11010052
